TPU v7x, 1024 devices: a whole 4x8x16 slice. The times are simulated.
1024 devices in a mesh: wide: 64 (over x, z_lo, core), narrow: 16 (over y, z_hi).
Axes of the slice: x: 4, y: 8, z: 16 (z_hi: 2, z_lo: 8; z = z_hi * 8 + z_lo), core: 2. Of those that a mesh axis runs over, the one named last changes fastest.
Arguments:
- activations: bfloat16 [131072, 4096], P(('wide', 'narrow')), may hold values from -6 to 6
- codes: bfloat16 [1024, 4, 512], P('narrow'), may hold values from -0.09375 to 0.09375
- scales: float32 [1024], P('narrow'), may hold values from 0.4 to 4
- cotangent: bfloat16 [131072, 512], P(('wide', 'narrow')), may hold values from -24 to 24
Outputs:
- values: bfloat16 [131072, 512], P(('wide', 'narrow'))
- input_grad: bfloat16 [131072, 4096], P(('wide', 'narrow'))
- weight_grad: float32 [4096, 512], P('narrow', 'wide')
All inputs are finite; a program needn't handle non-finite values.
Results may differ from a plain program's by a relative error of at most 0.017.
Values may be sent and summed in bfloat16 or wider, within the bound.
No kernel may reach another device: no remote copies, remote signals or barrier semaphores. Data moves between devices by JAX's collectives and lax.ppermute only.
A program may use at most 32 MiB of HBM per device.

v0:
```python
import math

import jax
import jax.numpy as jnp
from jax import lax
from jax.sharding import PartitionSpec as P


def body(activations, codes, scales, cotangent):
    width = codes.shape[2]
    group_size = lax.axis_size("narrow")
    tok_rows = activations.shape[0]
    factor = 1.0 / math.sqrt(tok_rows * lax.axis_size("wide") * group_size)
    code_piece = lax.all_gather(codes, "narrow", axis=0, tiled=True)
    scale_piece = lax.all_gather(scales.astype(jnp.bfloat16), "narrow", axis=0, tiled=True).astype(
        jnp.float32
    )
    dense = (
        (code_piece.astype(jnp.float32) * scale_piece[:, None, None])
        .astype(jnp.bfloat16)
        .reshape(-1, width)
    )
    values_sum = jnp.dot(activations, dense, preferred_element_type=jnp.float32)
    partial_grad = lax.dot_general(
        cotangent, dense, (((1,), (1,)), ((), ())), preferred_element_type=jnp.float32
    )
    grad_inputs = partial_grad
    values_sum, grad_inputs = (values_sum, grad_inputs)
    group_sum = lax.psum_scatter(
        (
            lax.dot_general(
                activations, cotangent, (((0,), (0,)), ((), ())), preferred_element_type=jnp.float32
            )
            * factor
        ).astype(jnp.bfloat16),
        "narrow",
        scatter_dimension=0,
        tiled=True,
    ).astype(jnp.float32)
    weight_grad = lax.psum_scatter(group_sum, "wide", scatter_dimension=1, tiled=True)
    return (values_sum.astype(jnp.bfloat16), grad_inputs.astype(jnp.bfloat16), weight_grad)


def solution(mesh):
    placed = (
        P(("wide", "narrow"), None),
        P("narrow", None, None),
        P("narrow"),
        P(("wide", "narrow"), None),
    )
    return jax.shard_map(
        body,
        mesh=mesh,
        in_specs=placed,
        out_specs=(P(("wide", "narrow"), None), P(("wide", "narrow"), None), P("narrow", "wide")),
        check_vma=False,
    )
```

profile of v0, /device:TPU:1, one launch (start us, length us, event | category | flops | bytes accessed | tf_op | source)
XLA Modules:
  0.0 949.4 jit_solution(5916628536034488836)
XLA Ops:
  7.2 0.0 copy-start
  7.2 0.0 reduce-scatter.5.cloned.1.call-start
  7.2 1.2 copy-done
  8.4 4.1 multiply_convert_fusion
  12.5 0.0 copy-start.2
  12.5 0.0 reduce-scatter.5.cloned.1.call-update
  12.6 0.0 all-gather.2.cloned.1.call-start
  12.6 0.7 all-gather.2.cloned.1.call-update
  13.3 0.0 reduce-scatter.7.cloned.1.call-start
  13.4 0.0 copy-done.2
  13.4 1.3 dynamic-slice
  15.3 0.2 dynamic-update-slice
  15.6 81.4 %all-reduce = bf16[1024]{0:T(1024)(128)(2,1)S(1)} all-reduce(bf16[1024]{0:T(1024)(128)(2,1)S(1)} %dynamic-update-slice), channel_id=1, replica_groups=mesh['wide'=64,'narrow'=16] {'narrow'}, use_global_device_ids=true, to_apply=%add | all-reduce | flops 1024 | bytes 4096
  97.0 224.5 %reduce-scatter.5.cloned.1.call-done = bf16[256,512]{1,0:T(8,128)(2,1)} async-done(((bf16[4096,512]{1,0:T(8,128)(2,1)}), bf16[256,512]{1,0:T(8,128)(2,1)}) %reduce-scatter.5.cloned.1.call-update) | async-done | bytes 262160 | tf_op jit(solution)/shard_map/reduce_scatter | solution.py:29
  321.5 1.9 copy.13
  323.4 0.0 reduce-scatter.7.cloned.1.call-update
  323.5 192.3 %all-gather.2.cloned.1.call-done = bf16[1024,4,512]{2,1,0:T(4,128)(2,1)} async-done(((bf16[64,4,512]{2,1,0:T(4,128)(2,1)}), bf16[1024,4,512]{2,1,0:T(4,128)(2,1)}) %all-gather.2.cloned.1.call-update) | async-done | bytes 4194320 | tf_op jit(solution)/shard_map/all_gather | solution.py:14
  515.8 6.2 multiply_convert_fusion.1
  522.0 0.0 copy-start.1
  522.0 6.9 reshape.10
  528.9 0.0 copy-done.1
  528.9 3.4 fusion
  532.4 1.3 copy.11
  533.7 3.5 fusion.1
  537.2 0.8 copy.10
  538.0 404.9 %reduce-scatter.7.cloned.1.call-done = f32[8,256]{1,0:T(8,128)} async-done(((f32[512,256]{1,0:T(8,128)}), f32[8,256]{1,0:T(8,128)}) %reduce-scatter.7.cloned.1.call-update) | async-done | bytes 8208
  (3 shorter events, 0.0 us)
Async XLA Ops:
  7.2 1.2 copy-start
  7.2 314.3 %reduce-scatter.5.cloned.1.call-start = ((), (), s32[]{:S(2)}) async-start(), calls=%async_computation.3 | async-start | bytes 4456448 | tf_op jit(solution)/shard_map/reduce_scatter | solution.py:29
  12.5 0.8 copy-start.2
  12.6 503.2 %all-gather.2.cloned.1.call-start = ((), (), s32[]{:S(2)}) async-start(), calls=%async_computation.2 | async-start | bytes 4456448 | tf_op jit(solution)/shard_map/all_gather | solution.py:14
  13.3 929.6 %reduce-scatter.7.cloned.1.call-start = ((), (), s32[]{:S(2)}) async-start(), calls=%async_computation.4 | async-start | bytes 532480
  522.0 6.9 copy-start.1
Sparse Core Ops, SparseCore 0:
  13.8 307.6 reduce-scatter.4
  325.9 189.8 all-gather.1
  519.7 423.1 reduce-scatter.6
where the time goes:
time: 958 us; the launch traced here: 949 us
  waiting for transfers between devices  823 us (86%)
  blocking collectives  81.4 us (8%)
  between operations  14.5 us (2%)
  local copies, waits for them, and re-layouts  13.6 us (1%)
  matrix products  11.1 us (1%)
    unnamed x4, waiting for transfers between devices  406 us
    reduce_scatter x1, waiting for transfers between devices, body(): lax.psum_scatter((lax.dot_general(activations, cotangent, (((0,), (0,)),...  225 us
    all_gather x1, waiting for transfers between devices, body(): code_piece = lax.all_gather(codes, 'narrow', axis=0, tiled=True)  192 us
    unnamed x1, blocking collectives  81.4 us
  transfers between devices with their start and end apart: 3, of which 3 were waited for; matrix products, arithmetic and copies ran while one was open for 3% of the time, Pallas kernels for 0%

commit v1 on v0

v1 whole, which is shorter than its diff:
```python
import math

import jax
import jax.numpy as jnp
from jax import lax
from jax.sharding import Mesh
from jax.sharding import PartitionSpec as P

AXES = ("x", "l", "c", "y", "h")
Z = ("h", "l")
SIZES = (4, 8, 2, 8, 2)


def dot(a, b, contract):
    return lax.dot_general(a, b, ((contract[:1], contract[1:]), ((), ())), preferred_element_type=jnp.float32)


def swap(value, axis):
    return lax.ppermute(value, axis, [(0, 1), (1, 0)])


def after(value, *others):
    return lax.optimization_barrier((value, *others))[0]


def body(activations, codes, scales, cotangent, factor):
    nx, nl, nc, ny, nh = (lax.axis_size(a) for a in AXES)
    tok, dw = activations.shape
    kv = cotangent.shape[1]
    ix, ic, ih = lax.axis_index("x"), lax.axis_index("c"), lax.axis_index("h")
    cols = kv // (nx * nl * nc)
    rows = dw // (ny * nh)

    count = codes.shape[0] // (nx * nc)
    first = (ix * nc + ic) * count
    code_part = lax.dynamic_slice_in_dim(codes, first, count, 0)
    scale_part = lax.dynamic_slice_in_dim(scales, first, count, 0)
    part = (code_part.astype(jnp.float32) * scale_part[:, None, None]).astype(jnp.bfloat16)
    part = part.reshape(-1, kv)
    part_rows = part.shape[0]
    other_part = swap(part, "h")

    half = kv // nc
    out_col = lax.broadcasted_iota(jnp.int32, (kv, half), 1)
    in_col = lax.broadcasted_iota(jnp.int32, (kv, half), 0)
    base_col = out_col + (out_col // cols) * cols

    def pick(core):
        chosen = (in_col == base_col + core * cols).astype(jnp.bfloat16)
        return dot(cotangent, chosen, (1, 0)).astype(jnp.bfloat16)

    cot_give = pick(1 - ic)
    act_other = swap(activations, "c")
    cot_other = swap(cot_give, "c")
    cot_keep = pick(ic)
    term = dot(cot_keep, activations, (0, 0))
    term = ((term + dot(cot_other, act_other, (0, 0))) * factor).astype(jnp.bfloat16)

    pair = jnp.where(ih == 0, jnp.stack([part, other_part]), jnp.stack([other_part, part]))
    copies = jnp.broadcast_to(pair[None], (ny,) + pair.shape)
    column = lax.all_to_all(copies, "y", 0, 0)

    term = after(term.reshape(nx, nl * cols, dw), column)
    got = lax.all_to_all(term, "x", 0, 0)
    total = jnp.sum(got.astype(jnp.float32), 0).astype(jnp.bfloat16)

    total = total.reshape(nl * cols, ny, nh * rows).transpose(1, 0, 2)
    got = lax.all_to_all(total, "y", 0, 0)
    total = jnp.sum(got.astype(jnp.float32), 0).astype(jnp.bfloat16)

    column = after(column, got)
    mine = lax.all_to_all(jnp.broadcast_to(column[None], (nx,) + column.shape), "x", 0, 0)
    theirs = swap(mine, "c")

    total = total.reshape(nl, cols, nh, rows).transpose(2, 0, 1, 3).reshape(nh * nl, cols, rows)
    got = lax.all_to_all(total, Z, 0, 0)
    weight_grad = jnp.sum(got.astype(jnp.float32), 0).T

    pair = jnp.where(ic == 0, jnp.stack([mine, theirs]), jnp.stack([theirs, mine]))
    dense = pair.transpose(2, 3, 1, 0, 4, 5).reshape(dw, kv)
    values = dot(activations, dense, (1, 0)).astype(jnp.bfloat16)
    grad_inputs = dot(cotangent, dense, (1, 1)).astype(jnp.bfloat16)
    return values, grad_inputs, weight_grad


def solution(mesh):
    fine = Mesh(mesh.devices.reshape(SIZES), AXES)
    wide, narrow = ("x", "l", "c"), ("y", "h")
    tokens = P(AXES, None)

    def run(activations, codes, scales, cotangent):
        factor = 1.0 / math.sqrt(activations.shape[0])
        return jax.shard_map(
            lambda *args: body(*args, factor),
            mesh=fine,
            in_specs=(tokens, P(narrow, None, None), P(narrow), tokens),
            out_specs=(tokens, tokens, P(narrow, wide)),
            check_vma=False,
        )(activations, codes, scales, cotangent)

    return run
```

time: 958 us -> 167 us (0.17)
  waiting for transfers between devices: 823 us -> 24.9 us
  starting transfers between devices: 0.12 us -> 48.2 us
  between operations: 14.5 us -> 0.85 us
  blocking collectives: 81.4 us -> 70.3 us
    unnamed x4 -> x0, waiting for transfers between devices: 406 us -> none
    reduce_scatter x1 -> x0, waiting for transfers between devices: 225 us -> none  [body(): lax.psum_scatter((lax.dot_general(activations, cotangent, (((0,), (0,)),...]
    all_gather x1 -> x0, waiting for transfers between devices: 192 us -> none  [body(): code_piece = lax.all_gather(codes, 'narrow', axis=0, tiled=True)]
    unnamed x1 -> x0, blocking collectives: 81.4 us -> none
    all_to_all x0 -> x3, blocking collectives: none -> 70.3 us  [the longest x1 28.4 us: body(): got = lax.all_to_all(term, 'x', 0, 0)]
    ppermute x0 -> x4, starting transfers between devices: none -> 32.4 us  [swap(): return lax.ppermute(value, axis, [(0, 1), (1, 0)])]
    all_to_all x0 -> x2, waiting for transfers between devices: none -> 18 us  [the longest x1 11.6 us: body(): got = lax.all_to_all(total, Z, 0, 0)]
    all_to_all x0 -> x2, starting transfers between devices: none -> 15.8 us  [the longest x1 12.3 us: body(): got = lax.all_to_all(total, Z, 0, 0)]
  transfers between devices with their start and end apart: 3 -> 6, of which waited for: 3 -> 3; matrix products, arithmetic and copies ran while one was open for 3% -> 7% of each run, Pallas kernels for 0% -> 0%
where the time goes in v1:
time: 167 us; the launch traced here: 166 us
  blocking collectives  70.3 us (42%)
  starting transfers between devices  48.2 us (29%)
  waiting for transfers between devices  24.9 us (15%)
  matrix products  10.2 us (6%)
  other arithmetic  6.28 us (4%)
  local copies, waits for them, and re-layouts  5.17 us (3%)
    ppermute x4, starting transfers between devices, swap(): return lax.ppermute(value, axis, [(0, 1), (1, 0)])  32.4 us
    all_to_all x1, blocking collectives, body(): got = lax.all_to_all(term, 'x', 0, 0)  28.4 us
    all_to_all x1, blocking collectives, body(): lax.all_to_all(jnp.broadcast_to(column[None], (nx,) + column.shape), 'x',...  25 us
    all_to_all x1, blocking collectives, body(): got = lax.all_to_all(total, 'y', 0, 0)  17 us
    all_to_all x1, starting transfers between devices, body(): got = lax.all_to_all(total, Z, 0, 0)  12.3 us
    all_to_all x1, waiting for transfers between devices, body(): got = lax.all_to_all(total, Z, 0, 0)  11.6 us
    dot_general x5, matrix products, dot(): lax.dot_general(a, b, ((contract[:1], contract[1:]), ((), ())), preferred...  10.2 us
    ppermute x4, waiting for transfers between devices, swap(): return lax.ppermute(value, axis, [(0, 1), (1, 0)])  6.89 us
  transfers between devices with their start and end apart: 6, of which 3 were waited for; matrix products, arithmetic and copies ran while one was open for 7% of the time, Pallas kernels for 0%

profile of v1, /device:TPU:1, one launch (start us, length us, event | category | flops | bytes accessed | tf_op | source)
XLA Modules:
  0.0 165.9 jit_solution(17658964175791954077)
XLA Ops:
  0.6 0.0 copy-start
  0.6 16.2 %collective-permute-start.2 = (bf16[128,4096]{1,0:T(8,128)(2,1)}, bf16[128,4096]{1,0:T(8,128)(2,1)}, u32[]{:S(2)}, u32[]{:S(2)}) collective-permute-start(bf16[128,4096]{1,0:T(8,128)(2,1)} %param.4), channel_id=1, source_target_pairs={{0,16},{16,0},{1,17},{17,1},{2,18},{18,2},{3,19},{19,3},{4,20},{20... | collective-permute-start | bytes 3145736 | tf_op jit(solution)/shard_map/ppermute | solution.py:19
  16.9 0.7 dynamic_slice.7
  17.6 0.8 multiply_convert_fusion
  18.5 6.4 %collective-permute-start = (bf16[32,512]{1,0:T(8,128)(2,1)S(1)}, bf16[32,512]{1,0:T(8,128)(2,1)S(1)}, u32[]{:S(2)}, u32[]{:S(2)}) collective-permute-start(bf16[32,512]{1,0:T(8,128)(2,1)S(1)} %reshape.59), channel_id=1, source_target_pairs={{0,1},{1,0},{2,3},{3,2},{4,5},{5,4},{6,7},{7,6},{8,9},{9,8},{10,11... | collective-permute-start | bytes 98312 | tf_op jit(solution)/shard_map/ppermute | solution.py:19
  24.9 6.9 %collective-permute-done = bf16[32,512]{1,0:T(8,128)(2,1)S(1)} collective-permute-done((bf16[32,512]{1,0:T(8,128)(2,1)S(1)}, bf16[32,512]{1,0:T(8,128)(2,1)S(1)}, u32[]{:S(2)}, u32[]{:S(2)}) %collective-permute-start) | collective-permute-done | bytes 32800 | tf_op jit(solution)/shard_map/ppermute | solution.py:19
  31.8 0.8 broadcast_in_dim.4
  32.7 3.5 %all-to-all-start = ((bf16[8,2,32,512]{3,2,1,0:T(8,128)(2,1)}), bf16[8,2,32,512]{3,2,1,0:T(8,128)(2,1)S(1)}, u32[]{:S(2)}, u32[]{:S(2)}) async-start(bf16[8,2,32,512]{3,2,1,0:T(8,128)(2,1)} %broadcast_in_dim.4), calls=%async_computation | async-start | bytes 1048576 | tf_op jit(solution)/shard_map/all_to_all | solution.py:61
  36.2 0.3 fusion.5
  36.5 3.1 %collective-permute-start.1 = (bf16[128,256]{0,1:T(8,128)(2,1)S(1)}, bf16[128,256]{0,1:T(8,128)(2,1)S(1)}, u32[]{:S(2)}, u32[]{:S(2)}) collective-permute-start(bf16[128,256]{0,1:T(8,128)(2,1)S(1)} %fusion.5), channel_id=1, source_target_pairs={{0,16},{16,0},{1,17},{17,1},{2,18},{18,2},{3,19},{19,3},{4,20},{20... | collective-permute-start | bytes 196616 | tf_op jit(solution)/shard_map/ppermute | solution.py:19
  39.6 4.2 %fusion.4 = f32[256,4096]{1,0:T(8,128)} fusion(bf16[128,4096]{1,0:T(8,128)(2,1)} %param.4, bf16[128,512]{1,0:T(8,128)(2,1)S(1)} %copy-done, s32[]{:T(128)S(6)} %mul.37, s32[256]{0:T(256)S(1)} %get-tuple-element.24, s32[256]{0:T(256)S(1)} %get-tuple-element.25, pred[256]{0:T(512)(128)(4,1)S(1)} %compare_and_fusion), kind=kOutput, calls=%fused_computation.10 | convolution fusion | flops 302809088 | bytes 5376260 | tf_op jit(solution)/shard_map/dot_general | solution.py:15
  43.7 3.2 %fusion.1 = bf16[256,4096]{1,0:T(8,128)(2,1)S(1)} fusion(f32[256,4096]{1,0:T(8,128)} %fusion.4, bf16[128,256]{0,1:T(8,128)(2,1)S(1)} %collective-permute-done.1, bf16[128,4096]{1,0:T(8,128)(2,1)} %collective-permute-done.2), kind=kOutput, calls=%fused_computation.2 | convolution fusion | flops 271581184 | bytes 7405568 | tf_op jit(solution)/shard_map/dot_general | solution.py:15
  47.0 6.4 %all-to-all-done = bf16[8,2,32,512]{3,2,1,0:T(8,128)(2,1)S(1)} async-done(((bf16[8,2,32,512]{3,2,1,0:T(8,128)(2,1)}), bf16[8,2,32,512]{3,2,1,0:T(8,128)(2,1)S(1)}, u32[]{:S(2)}, u32[]{:S(2)}) %all-to-all-start) | async-done | bytes 524320 | tf_op jit(solution)/shard_map/all_to_all | solution.py:61
  53.3 28.4 %all_to_all.25 = bf16[4,64,4096]{2,1,0:T(8,128)(2,1)} all-to-all(bf16[4,64,4096]{2,1,0:T(8,128)(2,1)S(1)} %bitcast.33), channel_id=1, replica_groups=mesh['x'=4,'l'=8,'c'=2,'y'=8,'h'=2] {'x'}, dimensions={0} | all-to-all | bytes 4194304 | tf_op jit(solution)/shard_map/all_to_all | solution.py:64
  81.7 2.0 %reduce_sum.33 = bf16[64,4096]{1,0:T(8,128)(2,1)S(1)} reduce(bf16[4,64,4096]{2,1,0:T(8,128)(2,1)} %all_to_all.25, bf16[]{:T(256)} %constant.45.clone.1), dimensions={0}, to_apply=%region_0.1 | reduce | flops 786432 | bytes 2621442 | tf_op jit(solution)/shard_map/reduce_sum | solution.py:65
  83.7 0.2 copy.25
  83.9 0.2 copy.19
  84.0 17.0 %all_to_all.26 = bf16[8,64,512]{2,1,0:T(8,128)(2,1)S(1)} all-to-all(bf16[8,64,512]{2,1,0:T(8,128)(2,1)S(1)} %copy.19), channel_id=1, replica_groups=mesh['x'=4,'l'=8,'c'=2,'y'=8,'h'=2] {'y'}, dimensions={0} | all-to-all | bytes 1048576 | tf_op jit(solution)/shard_map/all_to_all | solution.py:68
  101.0 0.2 broadcast_in_dim.5
  101.3 25.0 %all_to_all.27 = bf16[4,8,2,32,512]{4,3,2,1,0:T(8,128)(2,1)S(1)} all-to-all(bf16[4,8,2,32,512]{4,3,2,1,0:T(8,128)(2,1)S(1)} %broadcast_in_dim.5), channel_id=1, replica_groups=mesh['x'=4,'l'=8,'c'=2,'y'=8,'h'=2] {'x'}, dimensions={0} | all-to-all | bytes 4194304 | tf_op jit(solution)/shard_map/all_to_all | solution.py:72
  126.2 0.2 copy.28
  126.5 6.7 %collective-permute-start.3 = (bf16[4,8,2,32,512]{4,3,0,2,1:T(8,128)(2,1)S(1)}, bf16[4,8,2,32,512]{4,3,0,2,1:T(8,128)(2,1)}, u32[]{:S(2)}, u32[]{:S(2)}) collective-permute-start(bf16[4,8,2,32,512]{4,3,0,2,1:T(8,128)(2,1)S(1)} %copy.28), channel_id=1, source_target_pairs={{0,16},{16,0},{1,17},{17,1},{2,18},{18,2},{3,19},{19,3},{4,20},{20... | collective-permute-start | bytes 6291464 | tf_op jit(solution)/shard_map/ppermute | solution.py:19
  133.2 0.1 reduce_sum.34
  133.3 0.6 copy.22
  133.9 12.3 %all-to-all-start.4 = ((bf16[16,8,256]{2,1,0:T(8,128)(2,1)}), bf16[16,8,256]{2,1,0:T(8,128)(2,1)S(1)}, u32[]{:S(2)}, u32[]{:S(2)}) async-start(bf16[16,8,256]{2,1,0:T(8,128)(2,1)} %bitcast.12), calls=%async_computation.4 | async-start | bytes 131072 | tf_op jit(solution)/shard_map/all_to_all | solution.py:76
  146.2 11.6 %all-to-all-done.4 = bf16[16,8,256]{2,1,0:T(8,128)(2,1)S(1)} async-done(((bf16[16,8,256]{2,1,0:T(8,128)(2,1)}), bf16[16,8,256]{2,1,0:T(8,128)(2,1)S(1)}, u32[]{:S(2)}, u32[]{:S(2)}) %all-to-all-start.4) | async-done | bytes 65568 | tf_op jit(solution)/shard_map/all_to_all | solution.py:76
  157.9 0.6 convert_reduce_fusion
  158.5 2.8 %maximum_select_fusion = bf16[2,4,8,2,32,512]{5,4,0,1,3,2:T(8,128)(2,1)S(1)} fusion(bf16[1,4,8,2,32,512]{5,4,0,1,3,2:T(8,128)(2,1)} %bitcast.5, bf16[1,4,8,2,32,512]{5,4,0,1,3,2:T(8,128)(2,1)S(1)} %bitcast.34, pred[]{:T(512)S(6)} %eq.12), kind=kLoop, calls=%fused_computation.5 | loop fusion | flops 6291456 | bytes 8388609 | tf_op jit(solution)/shard_map/jit(_where)/select_n | solution.py:79
  161.3 1.3 fusion.3
  162.6 1.2 fusion.2
  163.8 1.3 copy.24
  165.1 0.8 copy.23
  (12 shorter events, 0.1 us)
Async XLA Ops:
  0.6 35.6 %copy-start = (bf16[128,512]{1,0:T(8,128)(2,1)S(1)}, bf16[128,512]{1,0:T(8,128)(2,1)}, u32[]{:S(2)}) copy-start(bf16[128,512]{1,0:T(8,128)(2,1)} %param.7) | copy-start | bytes 393220
  0.6 43.1 %collective-permute-start.2 = (bf16[128,4096]{1,0:T(8,128)(2,1)}, bf16[128,4096]{1,0:T(8,128)(2,1)}, u32[]{:S(2)}, u32[]{:S(2)}) collective-permute-start(bf16[128,4096]{1,0:T(8,128)(2,1)} %param.4), channel_id=1, source_target_pairs={{0,16},{16,0},{1,17},{17,1},{2,18},{18,2},{3,19},{19,3},{4,20},{20... | collective-permute-start | bytes 3145736 | tf_op jit(solution)/shard_map/ppermute | solution.py:19
  18.5 13.4 %collective-permute-start = (bf16[32,512]{1,0:T(8,128)(2,1)S(1)}, bf16[32,512]{1,0:T(8,128)(2,1)S(1)}, u32[]{:S(2)}, u32[]{:S(2)}) collective-permute-start(bf16[32,512]{1,0:T(8,128)(2,1)S(1)} %reshape.59), channel_id=1, source_target_pairs={{0,1},{1,0},{2,3},{3,2},{4,5},{5,4},{6,7},{7,6},{8,9},{9,8},{10,11... | collective-permute-start | bytes 98312 | tf_op jit(solution)/shard_map/ppermute | solution.py:19
  32.7 20.6 %all-to-all-start = ((bf16[8,2,32,512]{3,2,1,0:T(8,128)(2,1)}), bf16[8,2,32,512]{3,2,1,0:T(8,128)(2,1)S(1)}, u32[]{:S(2)}, u32[]{:S(2)}) async-start(bf16[8,2,32,512]{3,2,1,0:T(8,128)(2,1)} %broadcast_in_dim.4), calls=%async_computation | async-start | bytes 1048576 | tf_op jit(solution)/shard_map/all_to_all | solution.py:61
  36.5 7.3 %collective-permute-start.1 = (bf16[128,256]{0,1:T(8,128)(2,1)S(1)}, bf16[128,256]{0,1:T(8,128)(2,1)S(1)}, u32[]{:S(2)}, u32[]{:S(2)}) collective-permute-start(bf16[128,256]{0,1:T(8,128)(2,1)S(1)} %fusion.5), channel_id=1, source_target_pairs={{0,16},{16,0},{1,17},{17,1},{2,18},{18,2},{3,19},{19,3},{4,20},{20... | collective-permute-start | bytes 196616 | tf_op jit(solution)/shard_map/ppermute | solution.py:19
  126.5 32.0 %collective-permute-start.3 = (bf16[4,8,2,32,512]{4,3,0,2,1:T(8,128)(2,1)S(1)}, bf16[4,8,2,32,512]{4,3,0,2,1:T(8,128)(2,1)}, u32[]{:S(2)}, u32[]{:S(2)}) collective-permute-start(bf16[4,8,2,32,512]{4,3,0,2,1:T(8,128)(2,1)S(1)} %copy.28), channel_id=1, source_target_pairs={{0,16},{16,0},{1,17},{17,1},{2,18},{18,2},{3,19},{19,3},{4,20},{20... | collective-permute-start | bytes 6291464 | tf_op jit(solution)/shard_map/ppermute | solution.py:19
  133.9 24.0 %all-to-all-start.4 = ((bf16[16,8,256]{2,1,0:T(8,128)(2,1)}), bf16[16,8,256]{2,1,0:T(8,128)(2,1)S(1)}, u32[]{:S(2)}, u32[]{:S(2)}) async-start(bf16[16,8,256]{2,1,0:T(8,128)(2,1)} %bitcast.12), calls=%async_computation.4 | async-start | bytes 131072 | tf_op jit(solution)/shard_map/all_to_all | solution.py:76
  158.5 2.8 %copy-start.1 = (bf16[128,4096]{1,0:T(8,128)(2,1)S(1)}, bf16[128,4096]{1,0:T(8,128)(2,1)}, u32[]{:S(2)}) copy-start(bf16[128,4096]{1,0:T(8,128)(2,1)} %param.4) | copy-start | bytes 3145732

commit v2 on v1

v2 whole, which is shorter than its diff:
```python
import functools
import math

import jax
import jax.numpy as jnp
import numpy as np
from jax import lax
from jax.experimental import pallas as pl
from jax.experimental.pallas import tpu as pltpu
from jax.sharding import Mesh
from jax.sharding import PartitionSpec as P

AXES = ("x", "l", "c", "Y", "y", "h")
INTERPRET = False
SIZES = (4, 8, 2, 4, 2, 2)


def dot(a, b, contract):
    return lax.dot_general(a, b, ((contract[:1], contract[1:]), ((), ())), preferred_element_type=jnp.float32)


def swap(value, axis):
    return lax.ppermute(value, axis, [(0, 1), (1, 0)])


def after(value, *others):
    return lax.optimization_barrier((value, *others))[0]


def term_kernel(factor, keep_ref, other_ref, act_ref, act_other_ref, out_ref):
    both = dot(keep_ref[...], act_ref[...], (1, 0)) + dot(other_ref[...], act_other_ref[...], (1, 0))
    out_ref[...] = (both * factor).astype(out_ref.dtype).reshape(out_ref.shape)


def products(place, act_ref, cot_ref, mine_ref, theirs_ref, values_ref, grad_ref, dense_ref):
    ic, ih = place[0], place[1]
    ny, nh, height, _ = mine_ref.shape
    for dc, source in enumerate((mine_ref, theirs_ref)):
        c = lax.rem(ic + dc, 2)

        @pl.loop(0, ny)
        def _(y):
            for dh in range(nh):
                row = ((y * nh + lax.rem(ih + dh, nh)) * 2 + c) * height
                dense_ref[pl.ds(pl.multiple_of(row, height), height), :] = source[y, dh]

    values_ref[...] = dot(act_ref[...], dense_ref[...], (1, 0)).astype(values_ref.dtype)
    cot = cot_ref[...]
    step = min(512, dense_ref.shape[0])

    @pl.loop(0, dense_ref.shape[0] // step)
    def _(k):
        at = pl.ds(pl.multiple_of(k * step, step), step)
        grad_ref[:, at] = dot(cot, dense_ref[at, :], (1, 1)).astype(grad_ref.dtype)


def body(activations, codes, scales, cotangent, factor):
    nx, nl, nc, nY, ny, nh = (lax.axis_size(a) for a in AXES)
    tok, dw = activations.shape
    kv = cotangent.shape[1]
    ic, ih = lax.axis_index("c"), lax.axis_index("h")
    cols = kv // (nx * nl * nc)
    rows = dw // (nY * ny * nh)

    count = codes.shape[0] // nc
    first = ic * count
    code_part = lax.dynamic_slice_in_dim(codes, first, count, 0)
    scale_part = lax.dynamic_slice_in_dim(scales, first, count, 0)
    part = (code_part.astype(jnp.float32) * scale_part[:, None, None]).astype(jnp.bfloat16)
    part = part.reshape(-1, kv)

    half = kv // nc
    base = np.arange(kv, dtype=np.int32).reshape(nx * nl, nc, cols)[:, 0]
    base = base.reshape(half, 1)
    in_col = lax.broadcasted_iota(jnp.int32, (half, kv), 1)

    def pick(core):
        chosen = (in_col == base + core * cols).astype(jnp.bfloat16)
        return dot(chosen, cotangent, (1, 1)).astype(jnp.bfloat16)

    vmem = pl.BlockSpec(memory_space=pltpu.VMEM)
    act_other = swap(activations, "c")
    cot_other = swap(pick(1 - ic), "c")
    step = nh * rows
    parts = (nx, ny, nl * cols, nY * step)
    term = pl.pallas_call(
        functools.partial(term_kernel, factor),
        out_shape=jax.ShapeDtypeStruct(parts, jnp.bfloat16),
        grid=(dw // step,),
        in_specs=[pl.BlockSpec((half, tok), lambda k: (0, 0))] * 2 + [pl.BlockSpec((tok, step), lambda k: (0, k))] * 2,
        out_specs=pl.BlockSpec((nx, 1, nl * cols, step), lambda k: (0, k % ny, 0, k // ny)),
        compiler_params=pltpu.CompilerParams(vmem_limit_bytes=16 * 2**20),
        cost_estimate=pl.CostEstimate(flops=4 * tok * dw * half, bytes_accessed=8 * tok * dw, transcendentals=0),
        interpret=INTERPRET,
    )(pick(ic), cot_other, activations, act_other)

    pair = jnp.concatenate([part, swap(part, "h")])
    mine = lax.all_gather(pair, ("Y", "y"), axis=0, tiled=True)

    got = lax.all_to_all(term.reshape(nx * ny, *parts[2:]), ("x", "y"), 0, 0)
    total = jnp.sum(got.astype(jnp.float32), 0).astype(jnp.bfloat16)

    total = total.reshape(nl * cols, nY, step).transpose(1, 0, 2)
    got = lax.all_to_all(total, "Y", 0, 0)
    total = jnp.sum(got.astype(jnp.float32), 0).astype(jnp.bfloat16)

    total = total.reshape(nl, cols, nh, rows).transpose(2, 0, 1, 3).reshape(nh * nl, cols, rows)
    got = lax.all_to_all(total, ("h", "l"), 0, 0)
    weight_grad = jnp.sum(got.astype(jnp.float32), 0).T

    mine = after(mine, got)
    theirs = swap(mine, "c")

    place = jnp.stack([ic, ih]).astype(jnp.int32)
    blocks = (nY * ny, nh, part.shape[0], kv)
    values, grad_inputs = pl.pallas_call(
        products,
        out_shape=(
            jax.ShapeDtypeStruct((tok, kv), jnp.bfloat16),
            jax.ShapeDtypeStruct((tok, dw), jnp.bfloat16),
        ),
        in_specs=[pl.BlockSpec(memory_space=pltpu.SMEM), vmem, vmem, vmem, vmem],
        out_specs=(vmem, vmem),
        scratch_shapes=[pltpu.VMEM((dw, kv), jnp.bfloat16)],
        compiler_params=pltpu.CompilerParams(vmem_limit_bytes=24 * 2**20),
        cost_estimate=pl.CostEstimate(flops=4 * tok * dw * kv, bytes_accessed=4 * dw * kv, transcendentals=0),
        interpret=INTERPRET,
    )(place, activations, cotangent, mine.reshape(blocks), theirs.reshape(blocks))
    return values, grad_inputs, weight_grad


def solution(mesh):
    fine = Mesh(mesh.devices.reshape(SIZES), AXES)
    wide, narrow = AXES[:3], AXES[3:]
    tokens = P(AXES, None)

    def run(activations, codes, scales, cotangent):
        factor = 1.0 / math.sqrt(activations.shape[0])
        return jax.shard_map(
            lambda *args: body(*args, factor),
            mesh=fine,
            in_specs=(tokens, P(narrow, None, None), P(narrow), tokens),
            out_specs=(tokens, tokens, P(narrow, wide)),
            check_vma=False,
        )(activations, codes, scales, cotangent)

    return run
```

time: 167 us -> 128 us (0.77)
  blocking collectives: 70.3 us -> 10.8 us
  waiting for transfers between devices: 24.9 us -> 38.3 us
  between operations: 0.85 us -> 14.2 us
  Pallas kernels: 0 us -> 9.6 us
  matrix products: 10.2 us -> 2.36 us
  other arithmetic: 6.28 us -> 2.61 us
  starting transfers between devices: 48.2 us -> 46 us
    all_to_all x3 -> x1, blocking collectives: 70.3 us -> 10.8 us  [body(): got = lax.all_to_all(total, 'Y', 0, 0)]
    all_gather x0 -> x1, waiting for transfers between devices: none -> 17.4 us  [body(): mine = lax.all_gather(pair, ('Y', 'y'), axis=0, tiled=True)]
    pallas_call x0 -> x2, Pallas kernels: none -> 9.6 us  [the longest x1 5.09 us: body(): pl.pallas_call(products, out_shape=(jax.ShapeDtypeStruct((tok, kv), jnp.b...]
    dot_general x5 -> x2, matrix products: 10.2 us -> 2.36 us  [dot(): lax.dot_general(a, b, ((contract[:1], contract[1:]), ((), ())), preferred...]
    all_to_all x2, waiting for transfers between devices: 18 us -> 10.3 us  [the longest x1 10.3 us: body(): got = lax.all_to_all(term.reshape(nx * ny, *parts[2:]), ('x', 'y'), 0, 0)]
    ppermute x4, waiting for transfers between devices: 6.89 us -> 10.7 us  [swap(): return lax.ppermute(value, axis, [(0, 1), (1, 0)])]
    select_n x2 -> x0, other arithmetic: 2.76 us -> none  [the longest x1 2.75 us: body(): jnp.where(ic == 0, jnp.stack([mine, theirs]), jnp.stack([theirs, mine]))]
    all_to_all x2, starting transfers between devices: 15.8 us -> 14 us  [the longest x1 10.3 us: body(): got = lax.all_to_all(total, ('h', 'l'), 0, 0)]
  transfers between devices with their start and end apart: 6 -> 7, of which waited for: 3 -> 4; matrix products, arithmetic and copies ran while one was open for 7% -> 5% of each run, Pallas kernels for 0% -> 0%
where the time goes in v2:
time: 128 us
  starting transfers between devices  46 us (36%)
  waiting for transfers between devices  38.3 us (30%)
  between operations  14.2 us (11%)
  blocking collectives  10.8 us (8%)
  Pallas kernels  9.6 us (8%)
  local copies, waits for them, and re-layouts  3.84 us (3%)
  other arithmetic  2.61 us (2%)
  matrix products  2.36 us (2%)
    ppermute x4, starting transfers between devices, swap(): return lax.ppermute(value, axis, [(0, 1), (1, 0)])  32 us
    all_gather x1, waiting for transfers between devices, body(): mine = lax.all_gather(pair, ('Y', 'y'), axis=0, tiled=True)  17.4 us
    all_to_all x1, blocking collectives, body(): got = lax.all_to_all(total, 'Y', 0, 0)  10.8 us
    ppermute x4, waiting for transfers between devices, swap(): return lax.ppermute(value, axis, [(0, 1), (1, 0)])  10.7 us
    all_to_all x1, waiting for transfers between devices, body(): got = lax.all_to_all(term.reshape(nx * ny, *parts[2:]), ('x', 'y'), 0, 0)  10.3 us
    all_to_all x1, starting transfers between devices, body(): got = lax.all_to_all(total, ('h', 'l'), 0, 0)  10.3 us
    pallas_call x1, Pallas kernels, body(): pl.pallas_call(products, out_shape=(jax.ShapeDtypeStruct((tok, kv), jnp.b...  5.09 us
    pallas_call x1, Pallas kernels, body(): pl.pallas_call(functools.partial(term_kernel, factor), out_shape=jax.Shap...  4.5 us
  transfers between devices with their start and end apart: 7, of which 4 were waited for; matrix products, arithmetic and copies ran while one was open for 5% of the time, Pallas kernels for 0%

profile of v2, /device:TPU:1, one launch (start us, length us, event | category | flops | bytes accessed | tf_op | source)
XLA Modules:
  0.0 127.7 jit_solution(5981243068351297180)
XLA Ops:
  7.2 16.1 %collective-permute-start.2 = (bf16[128,4096]{1,0:T(8,128)(2,1)}, bf16[128,4096]{1,0:T(8,128)(2,1)S(1)}, u32[]{:S(2)}, u32[]{:S(2)}) collective-permute-start(bf16[128,4096]{1,0:T(8,128)(2,1)} %act_ref.3), channel_id=1, source_target_pairs={{0,16},{16,0},{1,17},{17,1},{2,18},{18,2},{3,19},{19,3},{4,20},{20... | collective-permute-start | bytes 3145736 | tf_op jit(solution)/shard_map/ppermute | solution.py:23
  23.2 0.7 broadcast_add_fusion
  23.9 1.2 convolution_convert_fusion
  25.1 1.9 %collective-permute-start.1 = (bf16[256,128]{1,0:T(8,128)(2,1)S(1)}, bf16[256,128]{1,0:T(8,128)(2,1)S(1)}, u32[]{:S(2)}, u32[]{:S(2)}) collective-permute-start(bf16[256,128]{1,0:T(8,128)(2,1)S(1)} %convolution_convert_fusion), channel_id=1, source_target_pairs={{0,16},{16,0},{1,17},{17,1},{2,18},{18,2},{3,19},{19,3},{4,20},{20... | collective-permute-start | bytes 196616 | tf_op jit(solution)/shard_map/ppermute | solution.py:23
  27.0 1.2 convolution_convert_fusion.1.keep_ref
  28.2 0.0 collective-permute-done.1.other_ref
  28.3 0.0 collective-permute-done.2.act_other_ref
  28.3 1.2 copy-done
  29.5 4.5 %shard_map.76 = bf16[4,2,64,2048]{3,2,1,0:T(8,128)(2,1)} custom-call(bf16[256,128]{1,0:T(8,128)(2,1)S(1)} %convolution_convert_fusion.1.keep_ref, bf16[256,128]{1,0:T(8,128)(2,1)S(1)} %collective-permute-done.1.other_ref, bf16[128,4096]{1,0:T(8,128)(2,1)S(1)} %copy-done, bf16[128,4096]{1,0:T(8,128)(2,1)S(1)} %collective-permute-done.2.act_other_ref), custom_call_target="tpu_custom_call" | custom-call | flops 536870912 | bytes 4194304 | tf_op jit(solution)/shard_map/pallas_call | solution.py:86
  34.0 3.7 %all-to-all-start = ((bf16[8,64,2048]{2,1,0:T(8,128)(2,1)}), bf16[8,64,2048]{2,1,0:T(8,128)(2,1)S(1)}, u32[]{:S(2)}, u32[]{:S(2)}) async-start(bf16[8,64,2048]{2,1,0:T(8,128)(2,1)} %bitcast.4), calls=%async_computation | async-start | bytes 4194304 | tf_op jit(solution)/shard_map/all_to_all | solution.py:100
  37.7 0.0 all-gather.2.cloned.1.call-start
  37.8 0.1 dynamic_slice.7
  37.9 0.1 multiply_convert_fusion
  38.0 7.8 %collective-permute-start = (bf16[128,512]{1,0:T(8,128)(2,1)S(1)}, bf16[128,512]{1,0:T(8,128)(2,1)S(1)}, u32[]{:S(2)}, u32[]{:S(2)}) collective-permute-start(bf16[128,512]{1,0:T(8,128)(2,1)S(1)} %reshape.28), channel_id=1, source_target_pairs={{0,1},{1,0},{2,3},{3,2},{4,5},{5,4},{6,7},{7,6},{8,9},{9,8},{10,11... | collective-permute-start | bytes 393224 | tf_op jit(solution)/shard_map/ppermute | solution.py:23
  45.9 7.4 %collective-permute-done = bf16[128,512]{1,0:T(8,128)(2,1)S(1)} collective-permute-done((bf16[128,512]{1,0:T(8,128)(2,1)S(1)}, bf16[128,512]{1,0:T(8,128)(2,1)S(1)}, u32[]{:S(2)}, u32[]{:S(2)}) %collective-permute-start) | collective-permute-done | bytes 131104 | tf_op jit(solution)/shard_map/ppermute | solution.py:23
  53.2 0.7 pad_maximum_fusion
  54.0 0.0 all-gather.2.cloned.1.call-update
  54.0 0.0 copy-start.1
  54.0 0.0 copy-start.3
  54.0 10.3 %all-to-all-done = bf16[8,64,2048]{2,1,0:T(8,128)(2,1)S(1)} async-done(((bf16[8,64,2048]{2,1,0:T(8,128)(2,1)}), bf16[8,64,2048]{2,1,0:T(8,128)(2,1)S(1)}, u32[]{:S(2)}, u32[]{:S(2)}) %all-to-all-start) | async-done | bytes 2097184 | tf_op jit(solution)/shard_map/all_to_all | solution.py:100
  64.3 0.4 reduce_sum.33
  64.6 0.2 reshape.30
  64.9 10.8 %all_to_all.15 = bf16[4,64,512]{2,1,0:T(8,128)(2,1)S(1)} all-to-all(bf16[4,64,512]{2,1,0:T(8,128)(2,1)S(1)} %copy.10), channel_id=1, replica_groups=mesh['x'=4,'l'=8,'c'=2,'Y'=4,'y'=2,'h'=2] {'Y'}, dimensions={0} | all-to-all | bytes 524288 | tf_op jit(solution)/shard_map/all_to_all | solution.py:104
  75.7 0.6 copy.11
  76.4 10.3 %all-to-all-start.2 = ((bf16[16,8,256]{2,1,0:T(8,128)(2,1)}), bf16[16,8,256]{2,1,0:T(8,128)(2,1)S(1)}, u32[]{:S(2)}, u32[]{:S(2)}) async-start(bf16[16,8,256]{2,1,0:T(8,128)(2,1)} %bitcast.7), calls=%async_computation.2 | async-start | bytes 131072 | tf_op jit(solution)/shard_map/all_to_all | solution.py:108
  86.6 17.4 %all-gather.2.cloned.1.call-done = bf16[2048,512]{1,0:T(8,128)(2,1)} async-done(((bf16[256,512]{1,0:T(8,128)(2,1)}), bf16[2048,512]{1,0:T(8,128)(2,1)}) %all-gather.2.cloned.1.call-update) | async-done | bytes 2097168 | tf_op jit(solution)/shard_map/all_gather | solution.py:98
  104.0 6.2 %collective-permute-start.3 = (bf16[2048,512]{1,0:T(8,128)(2,1)}, bf16[2048,512]{1,0:T(8,128)(2,1)S(1)}, u32[]{:S(2)}, u32[]{:S(2)}) collective-permute-start(bf16[2048,512]{1,0:T(8,128)(2,1)} %all-gather.2.cloned.1.call-done), channel_id=1, source_target_pairs={{0,16},{16,0},{1,17},{17,1},{2,18},{18,2},{3,19},{19,3},{4,20},{20... | collective-permute-start | bytes 6291464 | tf_op jit(solution)/shard_map/ppermute | solution.py:23
  110.2 0.1 pad_add_fusion.place
  110.2 0.6 convert_reduce_fusion
  110.9 3.3 %collective-permute-done.3 = bf16[2048,512]{1,0:T(8,128)(2,1)S(1)} collective-permute-done((bf16[2048,512]{1,0:T(8,128)(2,1)}, bf16[2048,512]{1,0:T(8,128)(2,1)S(1)}, u32[]{:S(2)}, u32[]{:S(2)}) %collective-permute-start.3) | collective-permute-done | bytes 2097184 | tf_op jit(solution)/shard_map/ppermute | solution.py:23
  114.1 1.6 %copy-done.2 = bf16[2048,512]{1,0:T(8,128)(2,1)S(1)} copy-done((bf16[2048,512]{1,0:T(8,128)(2,1)S(1)}, bf16[2048,512]{1,0:T(8,128)(2,1)}, u32[]{:S(2)}) %copy-start.2) | copy-done | bytes 2097176
  115.7 5.1 %shard_map.77 = (bf16[128,512]{1,0:T(8,128)(2,1)}, bf16[128,4096]{1,0:T(8,128)(2,1)}) custom-call(s32[2]{0:T(128)S(1)} %pad_add_fusion.place, bf16[128,4096]{1,0:T(8,128)(2,1)S(1)} %copy-done.1, bf16[128,512]{1,0:T(8,128)(2,1)S(1)} %copy-done.3, bf16[8,2,128,512]{3,2,1,0:T(8,128)(2,1)S(1)} %bitcast.13, bf16[8,2,128,512]{3,2,1,0:T(8,128)(2,1)S(1)} %bitcast.14), custom_call_target="tpu_custom_call" | custom-call | flops 1073741824 | bytes 8388608 | tf_op jit(solution)/shard_map/pallas_call | solution.py:116
  (13 shorter events, 0.2 us)
Async XLA Ops:
  7.2 21.1 %collective-permute-start.2 = (bf16[128,4096]{1,0:T(8,128)(2,1)}, bf16[128,4096]{1,0:T(8,128)(2,1)S(1)}, u32[]{:S(2)}, u32[]{:S(2)}) collective-permute-start(bf16[128,4096]{1,0:T(8,128)(2,1)} %act_ref.3), channel_id=1, source_target_pairs={{0,16},{16,0},{1,17},{17,1},{2,18},{18,2},{3,19},{19,3},{4,20},{20... | collective-permute-start | bytes 3145736 | tf_op jit(solution)/shard_map/ppermute | solution.py:23
  25.1 3.1 %collective-permute-start.1 = (bf16[256,128]{1,0:T(8,128)(2,1)S(1)}, bf16[256,128]{1,0:T(8,128)(2,1)S(1)}, u32[]{:S(2)}, u32[]{:S(2)}) collective-permute-start(bf16[256,128]{1,0:T(8,128)(2,1)S(1)} %convolution_convert_fusion), channel_id=1, source_target_pairs={{0,16},{16,0},{1,17},{17,1},{2,18},{18,2},{3,19},{19,3},{4,20},{20... | collective-permute-start | bytes 196616 | tf_op jit(solution)/shard_map/ppermute | solution.py:23
  28.3 1.2 copy-start
  34.0 3.8 %copy-start.5 = (f32[64]{0:T(128)S(1)}, f32[64]{0:T(128)}, u32[]{:S(2)}) copy-start(f32[64]{0:T(128)} %param.7) | copy-start | bytes 772
  34.0 3.9 %copy-start.4 = (bf16[64,4,512]{2,1,0:T(4,128)(2,1)S(1)}, bf16[64,4,512]{2,1,0:T(4,128)(2,1)}, u32[]{:S(2)}) copy-start(bf16[64,4,512]{2,1,0:T(4,128)(2,1)} %param.6) | copy-start | bytes 786436
  34.0 30.3 %all-to-all-start = ((bf16[8,64,2048]{2,1,0:T(8,128)(2,1)}), bf16[8,64,2048]{2,1,0:T(8,128)(2,1)S(1)}, u32[]{:S(2)}, u32[]{:S(2)}) async-start(bf16[8,64,2048]{2,1,0:T(8,128)(2,1)} %bitcast.4), calls=%async_computation | async-start | bytes 4194304 | tf_op jit(solution)/shard_map/all_to_all | solution.py:100
  37.7 66.3 %all-gather.2.cloned.1.call-start = ((), (), s32[]{:S(2)}) async-start(), calls=%async_computation.3 | async-start | bytes 2359296 | tf_op jit(solution)/shard_map/all_gather | solution.py:98
  38.0 15.2 %collective-permute-start = (bf16[128,512]{1,0:T(8,128)(2,1)S(1)}, bf16[128,512]{1,0:T(8,128)(2,1)S(1)}, u32[]{:S(2)}, u32[]{:S(2)}) collective-permute-start(bf16[128,512]{1,0:T(8,128)(2,1)S(1)} %reshape.28), channel_id=1, source_target_pairs={{0,1},{1,0},{2,3},{3,2},{4,5},{5,4},{6,7},{7,6},{8,9},{9,8},{10,11... | collective-permute-start | bytes 393224 | tf_op jit(solution)/shard_map/ppermute | solution.py:23
  54.0 60.1 %copy-start.1 = (bf16[128,4096]{1,0:T(8,128)(2,1)S(1)}, bf16[128,4096]{1,0:T(8,128)(2,1)}, u32[]{:S(2)}) copy-start(bf16[128,4096]{1,0:T(8,128)(2,1)} %act_ref.3) | copy-start | bytes 3145732
  54.0 60.1 %copy-start.3 = (bf16[128,512]{1,0:T(8,128)(2,1)S(1)}, bf16[128,512]{1,0:T(8,128)(2,1)}, u32[]{:S(2)}) copy-start(bf16[128,512]{1,0:T(8,128)(2,1)} %cot_ref.1) | copy-start | bytes 393220
  76.4 27.6 %all-to-all-start.2 = ((bf16[16,8,256]{2,1,0:T(8,128)(2,1)}), bf16[16,8,256]{2,1,0:T(8,128)(2,1)S(1)}, u32[]{:S(2)}, u32[]{:S(2)}) async-start(bf16[16,8,256]{2,1,0:T(8,128)(2,1)} %bitcast.7), calls=%async_computation.2 | async-start | bytes 131072 | tf_op jit(solution)/shard_map/all_to_all | solution.py:108
  104.0 10.1 %collective-permute-start.3 = (bf16[2048,512]{1,0:T(8,128)(2,1)}, bf16[2048,512]{1,0:T(8,128)(2,1)S(1)}, u32[]{:S(2)}, u32[]{:S(2)}) collective-permute-start(bf16[2048,512]{1,0:T(8,128)(2,1)} %all-gather.2.cloned.1.call-done), channel_id=1, source_target_pairs={{0,16},{16,0},{1,17},{17,1},{2,18},{18,2},{3,19},{19,3},{4,20},{20... | collective-permute-start | bytes 6291464 | tf_op jit(solution)/shard_map/ppermute | solution.py:23
  114.1 1.6 %copy-start.2 = (bf16[2048,512]{1,0:T(8,128)(2,1)S(1)}, bf16[2048,512]{1,0:T(8,128)(2,1)}, u32[]{:S(2)}) copy-start(bf16[2048,512]{1,0:T(8,128)(2,1)} %all-gather.2.cloned.1.call-done) | copy-start | bytes 6291460
Sparse Core Ops, SparseCore 0:
  54.1 49.8 all-gather.1

commit v3 on v2

--- a/solution.py
+++ b/solution.py
@@ -32,26 +32,45 @@
     out_ref[...] = (both * factor).astype(out_ref.dtype).reshape(out_ref.shape)
 
 
-def products(place, act_ref, cot_ref, mine_ref, theirs_ref, values_ref, grad_ref, dense_ref):
-    ic, ih = place[0], place[1]
-    ny, nh, height, _ = mine_ref.shape
-    for dc, source in enumerate((mine_ref, theirs_ref)):
-        c = lax.rem(ic + dc, 2)
+def half_products(core, place, act_ref, cot_ref, dense_ref, held_ref):
+    ny, nh, height, kv = dense_ref.shape
+    c = lax.rem(place[0] + core, 2)
 
-        @pl.loop(0, ny)
-        def _(y):
-            for dh in range(nh):
-                row = ((y * nh + lax.rem(ih + dh, nh)) * 2 + c) * height
-                dense_ref[pl.ds(pl.multiple_of(row, height), height), :] = source[y, dh]
+    def column(y, dh):
+        start = ((y * nh + lax.rem(place[1] + dh, nh)) * 2 + c) * height
+        return pl.ds(pl.multiple_of(start, height), height)
 
-    values_ref[...] = dot(act_ref[...], dense_ref[...], (1, 0)).astype(values_ref.dtype)
-    cot = cot_ref[...]
-    step = min(512, dense_ref.shape[0])
+    for y in range(ny):
+        for dh in range(nh):
+            held_ref[:, pl.ds((y * nh + dh) * height, height)] = act_ref[:, column(y, dh)]
+    total = dot(held_ref[...], dense_ref[...].reshape(ny * nh * height, kv), (1, 0))
 
-    @pl.loop(0, dense_ref.shape[0] // step)
-    def _(k):
-        at = pl.ds(pl.multiple_of(k * step, step), step)
-        grad_ref[:, at] = dot(cot, dense_ref[at, :], (1, 1)).astype(grad_ref.dtype)
+    def grad(y):
+        return dot(cot_ref[...], dense_ref[y].reshape(nh * height, kv), (1, 1)).astype(jnp.bfloat16)
+
+    return total, grad, column
+
+
+def own_kernel(place, act_ref, cot_ref, mine_ref, sum_ref, grad_ref, held_ref):
+    total, grad, _ = half_products(0, place, act_ref, cot_ref, mine_ref, held_ref)
+    sum_ref[...] = total
+    for y in range(mine_ref.shape[0]):
+        grad_ref[y] = grad(y)
+
+
+def other_kernel(place, act_ref, cot_ref, theirs_ref, sum_ref, own_ref, values_ref, grad_ref, held_ref):
+    total, grad, column = half_products(1, place, act_ref, cot_ref, theirs_ref, held_ref)
+    values_ref[...] = (total + sum_ref[...]).astype(values_ref.dtype)
+    ny, nh, height, _ = theirs_ref.shape
+    for y in range(ny):
+        piece = grad(y)
+        for dh in range(nh):
+            at = pl.ds(dh * height, height)
+            other = column(y, dh)
+            grad_ref[:, other] = piece[:, dh * height : (dh + 1) * height]
+            c = lax.rem(place[0], 2)
+            start = ((y * nh + lax.rem(place[1] + dh, nh)) * 2 + c) * height
+            grad_ref[:, pl.ds(pl.multiple_of(start, height), height)] = own_ref[y, :, at]
 
 
 def body(activations, codes, scales, cotangent, factor):
@@ -113,19 +132,31 @@
 
     place = jnp.stack([ic, ih]).astype(jnp.int32)
     blocks = (nY * ny, nh, part.shape[0], kv)
-    values, grad_inputs = pl.pallas_call(
-        products,
-        out_shape=(
-            jax.ShapeDtypeStruct((tok, kv), jnp.bfloat16),
-            jax.ShapeDtypeStruct((tok, dw), jnp.bfloat16),
-        ),
-        in_specs=[pl.BlockSpec(memory_space=pltpu.SMEM), vmem, vmem, vmem, vmem],
-        out_specs=(vmem, vmem),
-        scratch_shapes=[pltpu.VMEM((dw, kv), jnp.bfloat16)],
-        compiler_params=pltpu.CompilerParams(vmem_limit_bytes=24 * 2**20),
-        cost_estimate=pl.CostEstimate(flops=4 * tok * dw * kv, bytes_accessed=4 * dw * kv, transcendentals=0),
-        interpret=INTERPRET,
-    )(place, activations, cotangent, mine.reshape(blocks), theirs.reshape(blocks))
+    smem = pl.BlockSpec(memory_space=pltpu.SMEM)
+    width = dw // nc
+
+    def kernel(body, outs, operands):
+        return pl.pallas_call(
+            body,
+            out_shape=tuple(jax.ShapeDtypeStruct(*out) for out in outs),
+            in_specs=[smem] + [vmem] * len(operands),
+            out_specs=(vmem, vmem),
+            scratch_shapes=[pltpu.VMEM((tok, width), jnp.bfloat16)],
+            compiler_params=pltpu.CompilerParams(vmem_limit_bytes=24 * 2**20),
+            cost_estimate=pl.CostEstimate(flops=2 * tok * dw * kv, bytes_accessed=2 * dw * kv, transcendentals=0),
+            interpret=INTERPRET,
+        )(place, *operands)
+
+    own_sum, own_grad = kernel(
+        own_kernel,
+        [((tok, kv), jnp.float32), ((blocks[0], tok, width // blocks[0]), jnp.bfloat16)],
+        (activations, cotangent, mine.reshape(blocks)),
+    )
+    values, grad_inputs = kernel(
+        other_kernel,
+        [((tok, kv), jnp.bfloat16), ((tok, dw), jnp.bfloat16)],
+        (activations, cotangent, theirs.reshape(blocks), own_sum, own_grad),
+    )
     return values, grad_inputs, weight_grad
 
 

time: 128 us -> 124 us (0.969)
  waiting for transfers between devices: 38.3 us -> 35 us
    ppermute x4, waiting for transfers between devices: 10.7 us -> 7.39 us  [swap(): return lax.ppermute(value, axis, [(0, 1), (1, 0)])]
    pallas_call x1 -> x2, Pallas kernels: 5.09 us -> 4.43 us  [kernel(): pl.pallas_call(body, out_shape=tuple((jax.ShapeDtypeStruct(*out) for out...]
  transfers between devices with their start and end apart: 7 -> 7, of which waited for: 4 -> 3; matrix products, arithmetic and copies ran while one was open for 5% -> 5% of each run, Pallas kernels for 0% -> 1%
where the time goes in v3:
time: 124 us
  starting transfers between devices  46.1 us (37%)
  waiting for transfers between devices  35 us (28%)
  between operations  14.2 us (11%)
  blocking collectives  10.8 us (9%)
  Pallas kernels  8.93 us (7%)
  local copies, waits for them, and re-layouts  3.84 us (3%)
  other arithmetic  2.62 us (2%)
  matrix products  2.36 us (2%)
    ppermute x4, starting transfers between devices, swap(): return lax.ppermute(value, axis, [(0, 1), (1, 0)])  32 us
    all_gather x1, waiting for transfers between devices, body(): mine = lax.all_gather(pair, ('Y', 'y'), axis=0, tiled=True)  17.4 us
    all_to_all x1, blocking collectives, body(): got = lax.all_to_all(total, 'Y', 0, 0)  10.8 us
    all_to_all x1, starting transfers between devices, body(): got = lax.all_to_all(total, ('h', 'l'), 0, 0)  10.3 us
    all_to_all x1, waiting for transfers between devices, body(): got = lax.all_to_all(term.reshape(nx * ny, *parts[2:]), ('x', 'y'), 0, 0)  10.3 us
    ppermute x4, waiting for transfers between devices, swap(): return lax.ppermute(value, axis, [(0, 1), (1, 0)])  7.39 us
    pallas_call x1, Pallas kernels, body(): pl.pallas_call(functools.partial(term_kernel, factor), out_shape=jax.Shap...  4.51 us
    pallas_call x2, Pallas kernels, kernel(): pl.pallas_call(body, out_shape=tuple((jax.ShapeDtypeStruct(*out) for out...  4.43 us
  transfers between devices with their start and end apart: 7, of which 3 were waited for; matrix products, arithmetic and copies ran while one was open for 5% of the time, Pallas kernels for 1%

profile of v3, /device:TPU:1, one launch (start us, length us, event | category | flops | bytes accessed | tf_op | source)
XLA Modules:
  0.0 123.8 jit_solution(4782120235804046980)
XLA Ops:
  7.2 16.1 %collective-permute-start.2 = (bf16[128,4096]{1,0:T(8,128)(2,1)}, bf16[128,4096]{1,0:T(8,128)(2,1)S(1)}, u32[]{:S(2)}, u32[]{:S(2)}) collective-permute-start(bf16[128,4096]{1,0:T(8,128)(2,1)} %act_ref.5), channel_id=1, source_target_pairs={{0,16},{16,0},{1,17},{17,1},{2,18},{18,2},{3,19},{19,3},{4,20},{20... | collective-permute-start | bytes 3145736 | tf_op jit(solution)/shard_map/ppermute | solution.py:23
  23.2 0.7 broadcast_add_fusion
  23.9 1.2 convolution_convert_fusion
  25.1 1.9 %collective-permute-start.1 = (bf16[256,128]{1,0:T(8,128)(2,1)S(1)}, bf16[256,128]{1,0:T(8,128)(2,1)S(1)}, u32[]{:S(2)}, u32[]{:S(2)}) collective-permute-start(bf16[256,128]{1,0:T(8,128)(2,1)S(1)} %convolution_convert_fusion), channel_id=1, source_target_pairs={{0,16},{16,0},{1,17},{17,1},{2,18},{18,2},{3,19},{19,3},{4,20},{20... | collective-permute-start | bytes 196616 | tf_op jit(solution)/shard_map/ppermute | solution.py:23
  27.0 1.2 convolution_convert_fusion.1.keep_ref
  28.2 0.0 collective-permute-done.1.other_ref
  28.3 1.2 copy-done
  29.5 4.5 %shard_map.76 = bf16[4,2,64,2048]{3,2,1,0:T(8,128)(2,1)} custom-call(bf16[256,128]{1,0:T(8,128)(2,1)S(1)} %convolution_convert_fusion.1.keep_ref, bf16[256,128]{1,0:T(8,128)(2,1)S(1)} %collective-permute-done.1.other_ref, bf16[128,4096]{1,0:T(8,128)(2,1)S(1)} %copy-done, bf16[128,4096]{1,0:T(8,128)(2,1)S(1)} %collective-permute-done.2.act_other_ref), custom_call_target="tpu_custom_call" | custom-call | flops 536870912 | bytes 4194304 | tf_op jit(solution)/shard_map/pallas_call | solution.py:105
  34.0 3.7 %all-to-all-start = ((bf16[8,64,2048]{2,1,0:T(8,128)(2,1)}), bf16[8,64,2048]{2,1,0:T(8,128)(2,1)S(1)}, u32[]{:S(2)}, u32[]{:S(2)}) async-start(bf16[8,64,2048]{2,1,0:T(8,128)(2,1)} %bitcast.4), calls=%async_computation | async-start | bytes 4194304 | tf_op jit(solution)/shard_map/all_to_all | solution.py:119
  37.7 0.0 all-gather.2.cloned.1.call-start
  37.8 0.1 dynamic_slice.7
  37.9 0.1 multiply_convert_fusion
  38.0 7.8 %collective-permute-start = (bf16[128,512]{1,0:T(8,128)(2,1)S(1)}, bf16[128,512]{1,0:T(8,128)(2,1)S(1)}, u32[]{:S(2)}, u32[]{:S(2)}) collective-permute-start(bf16[128,512]{1,0:T(8,128)(2,1)S(1)} %reshape.28), channel_id=1, source_target_pairs={{0,1},{1,0},{2,3},{3,2},{4,5},{5,4},{6,7},{7,6},{8,9},{9,8},{10,11... | collective-permute-start | bytes 393224 | tf_op jit(solution)/shard_map/ppermute | solution.py:23
  45.9 7.4 %collective-permute-done = bf16[128,512]{1,0:T(8,128)(2,1)S(1)} collective-permute-done((bf16[128,512]{1,0:T(8,128)(2,1)S(1)}, bf16[128,512]{1,0:T(8,128)(2,1)S(1)}, u32[]{:S(2)}, u32[]{:S(2)}) %collective-permute-start) | collective-permute-done | bytes 131104 | tf_op jit(solution)/shard_map/ppermute | solution.py:23
  53.3 0.7 pad_maximum_fusion
  54.0 0.0 all-gather.2.cloned.1.call-update
  54.0 0.0 copy-start.1
  54.0 0.0 copy-start.3
  54.0 10.3 %all-to-all-done = bf16[8,64,2048]{2,1,0:T(8,128)(2,1)S(1)} async-done(((bf16[8,64,2048]{2,1,0:T(8,128)(2,1)}), bf16[8,64,2048]{2,1,0:T(8,128)(2,1)S(1)}, u32[]{:S(2)}, u32[]{:S(2)}) %all-to-all-start) | async-done | bytes 2097184 | tf_op jit(solution)/shard_map/all_to_all | solution.py:119
  64.3 0.4 reduce_sum.33
  64.6 0.2 reshape.30
  64.9 10.8 %all_to_all.15 = bf16[4,64,512]{2,1,0:T(8,128)(2,1)S(1)} all-to-all(bf16[4,64,512]{2,1,0:T(8,128)(2,1)S(1)} %copy.10), channel_id=1, replica_groups=mesh['x'=4,'l'=8,'c'=2,'Y'=4,'y'=2,'h'=2] {'Y'}, dimensions={0} | all-to-all | bytes 524288 | tf_op jit(solution)/shard_map/all_to_all | solution.py:123
  75.7 0.6 copy.11
  76.4 10.3 %all-to-all-start.2 = ((bf16[16,8,256]{2,1,0:T(8,128)(2,1)}), bf16[16,8,256]{2,1,0:T(8,128)(2,1)S(1)}, u32[]{:S(2)}, u32[]{:S(2)}) async-start(bf16[16,8,256]{2,1,0:T(8,128)(2,1)} %bitcast.7), calls=%async_computation.2 | async-start | bytes 131072 | tf_op jit(solution)/shard_map/all_to_all | solution.py:127
  86.6 17.4 %all-gather.2.cloned.1.call-done = bf16[2048,512]{1,0:T(8,128)(2,1)} async-done(((bf16[256,512]{1,0:T(8,128)(2,1)}), bf16[2048,512]{1,0:T(8,128)(2,1)}) %all-gather.2.cloned.1.call-update) | async-done | bytes 2097168 | tf_op jit(solution)/shard_map/all_gather | solution.py:117
  104.0 6.2 %collective-permute-start.3 = (bf16[2048,512]{1,0:T(8,128)(2,1)}, bf16[2048,512]{1,0:T(8,128)(2,1)S(1)}, u32[]{:S(2)}, u32[]{:S(2)}) collective-permute-start(bf16[2048,512]{1,0:T(8,128)(2,1)} %all-gather.2.cloned.1.call-done), channel_id=1, source_target_pairs={{0,16},{16,0},{1,17},{17,1},{2,18},{18,2},{3,19},{19,3},{4,20},{20... | collective-permute-start | bytes 6291464 | tf_op jit(solution)/shard_map/ppermute | solution.py:23
  110.2 0.1 pad_add_fusion.place
  110.3 1.6 %copy-done.2 = bf16[2048,512]{1,0:T(8,128)(2,1)S(1)} copy-done((bf16[2048,512]{1,0:T(8,128)(2,1)S(1)}, bf16[2048,512]{1,0:T(8,128)(2,1)}, u32[]{:S(2)}) %copy-start.2) | copy-done | bytes 2097176
  111.9 1.7 %shard_map.77 = (f32[128,512]{1,0:T(8,128)S(1)}, bf16[8,128,256]{2,1,0:T(8,128)(2,1)S(1)}) custom-call(s32[2]{0:T(128)S(1)} %pad_add_fusion.place, bf16[128,4096]{1,0:T(8,128)(2,1)S(1)} %copy-done.1, bf16[128,512]{1,0:T(8,128)(2,1)S(1)} %copy-done.3, bf16[8,2,128,512]{3,2,1,0:T(8,128)(2,1)S(1)} %bitcast.13), custom_call_target="tpu_custom_call" | custom-call | flops 536870912 | bytes 4194304 | tf_op jit(solution)/shard_map/pallas_call | solution.py:139
  113.6 0.6 convert_reduce_fusion
  114.2 0.0 collective-permute-done.3
  114.2 2.7 %shard_map.78 = (bf16[128,512]{1,0:T(8,128)(2,1)}, bf16[128,4096]{1,0:T(8,128)(2,1)}) custom-call(s32[2]{0:T(128)S(1)} %pad_add_fusion.place, bf16[128,4096]{1,0:T(8,128)(2,1)S(1)} %copy-done.1, bf16[128,512]{1,0:T(8,128)(2,1)S(1)} %copy-done.3, bf16[8,2,128,512]{3,2,1,0:T(8,128)(2,1)S(1)} %bitcast.14, f32[128,512]{1,0:T(8,128)S(1)} %get-tuple-element.9.sum_ref, ...), custom_call_target="tpu_custom_call" | custom-call | flops 536870912 | bytes 4194304 | tf_op jit(solution)/shard_map/pallas_call | solution.py:139
  (14 shorter events, 0.2 us)
Async XLA Ops:
  7.2 21.1 %collective-permute-start.2 = (bf16[128,4096]{1,0:T(8,128)(2,1)}, bf16[128,4096]{1,0:T(8,128)(2,1)S(1)}, u32[]{:S(2)}, u32[]{:S(2)}) collective-permute-start(bf16[128,4096]{1,0:T(8,128)(2,1)} %act_ref.5), channel_id=1, source_target_pairs={{0,16},{16,0},{1,17},{17,1},{2,18},{18,2},{3,19},{19,3},{4,20},{20... | collective-permute-start | bytes 3145736 | tf_op jit(solution)/shard_map/ppermute | solution.py:23
  25.1 3.1 %collective-permute-start.1 = (bf16[256,128]{1,0:T(8,128)(2,1)S(1)}, bf16[256,128]{1,0:T(8,128)(2,1)S(1)}, u32[]{:S(2)}, u32[]{:S(2)}) collective-permute-start(bf16[256,128]{1,0:T(8,128)(2,1)S(1)} %convolution_convert_fusion), channel_id=1, source_target_pairs={{0,16},{16,0},{1,17},{17,1},{2,18},{18,2},{3,19},{19,3},{4,20},{20... | collective-permute-start | bytes 196616 | tf_op jit(solution)/shard_map/ppermute | solution.py:23
  28.3 1.2 copy-start
  34.0 3.8 %copy-start.5 = (f32[64]{0:T(128)S(1)}, f32[64]{0:T(128)}, u32[]{:S(2)}) copy-start(f32[64]{0:T(128)} %param.7) | copy-start | bytes 772
  34.0 3.9 %copy-start.4 = (bf16[64,4,512]{2,1,0:T(4,128)(2,1)S(1)}, bf16[64,4,512]{2,1,0:T(4,128)(2,1)}, u32[]{:S(2)}) copy-start(bf16[64,4,512]{2,1,0:T(4,128)(2,1)} %param.6) | copy-start | bytes 786436
  34.0 30.3 %all-to-all-start = ((bf16[8,64,2048]{2,1,0:T(8,128)(2,1)}), bf16[8,64,2048]{2,1,0:T(8,128)(2,1)S(1)}, u32[]{:S(2)}, u32[]{:S(2)}) async-start(bf16[8,64,2048]{2,1,0:T(8,128)(2,1)} %bitcast.4), calls=%async_computation | async-start | bytes 4194304 | tf_op jit(solution)/shard_map/all_to_all | solution.py:119
  37.7 66.3 %all-gather.2.cloned.1.call-start = ((), (), s32[]{:S(2)}) async-start(), calls=%async_computation.3 | async-start | bytes 2359296 | tf_op jit(solution)/shard_map/all_gather | solution.py:117
  38.0 15.2 %collective-permute-start = (bf16[128,512]{1,0:T(8,128)(2,1)S(1)}, bf16[128,512]{1,0:T(8,128)(2,1)S(1)}, u32[]{:S(2)}, u32[]{:S(2)}) collective-permute-start(bf16[128,512]{1,0:T(8,128)(2,1)S(1)} %reshape.28), channel_id=1, source_target_pairs={{0,1},{1,0},{2,3},{3,2},{4,5},{5,4},{6,7},{7,6},{8,9},{9,8},{10,11... | collective-permute-start | bytes 393224 | tf_op jit(solution)/shard_map/ppermute | solution.py:23
  54.0 56.3 %copy-start.1 = (bf16[128,4096]{1,0:T(8,128)(2,1)S(1)}, bf16[128,4096]{1,0:T(8,128)(2,1)}, u32[]{:S(2)}) copy-start(bf16[128,4096]{1,0:T(8,128)(2,1)} %act_ref.5) | copy-start | bytes 3145732
  54.0 56.3 %copy-start.3 = (bf16[128,512]{1,0:T(8,128)(2,1)S(1)}, bf16[128,512]{1,0:T(8,128)(2,1)}, u32[]{:S(2)}) copy-start(bf16[128,512]{1,0:T(8,128)(2,1)} %cot_ref.3) | copy-start | bytes 393220
  76.4 27.6 %all-to-all-start.2 = ((bf16[16,8,256]{2,1,0:T(8,128)(2,1)}), bf16[16,8,256]{2,1,0:T(8,128)(2,1)S(1)}, u32[]{:S(2)}, u32[]{:S(2)}) async-start(bf16[16,8,256]{2,1,0:T(8,128)(2,1)} %bitcast.7), calls=%async_computation.2 | async-start | bytes 131072 | tf_op jit(solution)/shard_map/all_to_all | solution.py:127
  104.0 10.2 %collective-permute-start.3 = (bf16[2048,512]{1,0:T(8,128)(2,1)}, bf16[2048,512]{1,0:T(8,128)(2,1)S(1)}, u32[]{:S(2)}, u32[]{:S(2)}) collective-permute-start(bf16[2048,512]{1,0:T(8,128)(2,1)} %all-gather.2.cloned.1.call-done), channel_id=1, source_target_pairs={{0,16},{16,0},{1,17},{17,1},{2,18},{18,2},{3,19},{19,3},{4,20},{20... | collective-permute-start | bytes 6291464 | tf_op jit(solution)/shard_map/ppermute | solution.py:23
  110.3 1.6 %copy-start.2 = (bf16[2048,512]{1,0:T(8,128)(2,1)S(1)}, bf16[2048,512]{1,0:T(8,128)(2,1)}, u32[]{:S(2)}) copy-start(bf16[2048,512]{1,0:T(8,128)(2,1)} %all-gather.2.cloned.1.call-done) | copy-start | bytes 6291460
Sparse Core Ops, SparseCore 0:
  54.1 49.8 all-gather.1

commit v4 on v3

--- a/solution.py
+++ b/solution.py
@@ -27,9 +27,13 @@
     return lax.optimization_barrier((value, *others))[0]
 
 
-def term_kernel(factor, keep_ref, other_ref, act_ref, act_other_ref, out_ref):
-    both = dot(keep_ref[...], act_ref[...], (1, 0)) + dot(other_ref[...], act_other_ref[...], (1, 0))
-    out_ref[...] = (both * factor).astype(out_ref.dtype).reshape(out_ref.shape)
+def term_kernel(factor, step, keep_ref, other_ref, act_ref, act_other_ref, out_ref):
+    nx, ny, height, width = out_ref.shape
+    for k in range(act_ref.shape[1] // step):
+        at = pl.ds(k * step, step)
+        both = dot(keep_ref[...], act_ref[:, at], (1, 0)) + dot(other_ref[...], act_other_ref[:, at], (1, 0))
+        piece = (both * factor).astype(out_ref.dtype).reshape(nx, height, step)
+        out_ref[:, k % ny, :, pl.ds(k // ny * step, step)] = piece
 
 
 def half_products(core, place, act_ref, cot_ref, dense_ref, held_ref):
@@ -103,11 +107,10 @@
     step = nh * rows
     parts = (nx, ny, nl * cols, nY * step)
     term = pl.pallas_call(
-        functools.partial(term_kernel, factor),
+        functools.partial(term_kernel, factor, step),
         out_shape=jax.ShapeDtypeStruct(parts, jnp.bfloat16),
-        grid=(dw // step,),
-        in_specs=[pl.BlockSpec((half, tok), lambda k: (0, 0))] * 2 + [pl.BlockSpec((tok, step), lambda k: (0, k))] * 2,
-        out_specs=pl.BlockSpec((nx, 1, nl * cols, step), lambda k: (0, k % ny, 0, k // ny)),
+        in_specs=[vmem] * 4,
+        out_specs=vmem,
         compiler_params=pltpu.CompilerParams(vmem_limit_bytes=16 * 2**20),
         cost_estimate=pl.CostEstimate(flops=4 * tok * dw * half, bytes_accessed=8 * tok * dw, transcendentals=0),
         interpret=INTERPRET,

time: 124 us -> 122 us (0.984)
  Pallas kernels: 8.93 us -> 6.98 us
    pallas_call x1, Pallas kernels: 4.51 us -> 2.55 us  [body(): pl.pallas_call(functools.partial(term_kernel, factor, step), out_shape=ja...]
where the time goes in v4:
time: 122 us
  starting transfers between devices  46.1 us (38%)
  waiting for transfers between devices  35 us (29%)
  between operations  14.2 us (12%)
  blocking collectives  10.8 us (9%)
  Pallas kernels  6.98 us (6%)
  local copies, waits for them, and re-layouts  3.84 us (3%)
  other arithmetic  2.62 us (2%)
  matrix products  2.36 us (2%)
    ppermute x4, starting transfers between devices, swap(): return lax.ppermute(value, axis, [(0, 1), (1, 0)])  32 us
    all_gather x1, waiting for transfers between devices, body(): mine = lax.all_gather(pair, ('Y', 'y'), axis=0, tiled=True)  17.4 us
    all_to_all x1, blocking collectives, body(): got = lax.all_to_all(total, 'Y', 0, 0)  10.8 us
    all_to_all x1, starting transfers between devices, body(): got = lax.all_to_all(total, ('h', 'l'), 0, 0)  10.3 us
    all_to_all x1, waiting for transfers between devices, body(): got = lax.all_to_all(term.reshape(nx * ny, *parts[2:]), ('x', 'y'), 0, 0)  10.3 us
    ppermute x4, waiting for transfers between devices, swap(): return lax.ppermute(value, axis, [(0, 1), (1, 0)])  7.39 us
    pallas_call x2, Pallas kernels, kernel(): pl.pallas_call(body, out_shape=tuple((jax.ShapeDtypeStruct(*out) for out...  4.43 us
    all_to_all x1, starting transfers between devices, body(): got = lax.all_to_all(term.reshape(nx * ny, *parts[2:]), ('x', 'y'), 0, 0)  3.73 us
  transfers between devices with their start and end apart: 7, of which 3 were waited for; matrix products, arithmetic and copies ran while one was open for 5% of the time, Pallas kernels for 1%

profile of v4, /device:TPU:1, one launch (start us, length us, event | category | flops | bytes accessed | tf_op | source)
XLA Modules:
  0.0 121.8 jit_solution(6956121283061354040)
XLA Ops:
  7.2 16.1 %collective-permute-start.2 = (bf16[128,4096]{1,0:T(8,128)(2,1)}, bf16[128,4096]{1,0:T(8,128)(2,1)S(1)}, u32[]{:S(2)}, u32[]{:S(2)}) collective-permute-start(bf16[128,4096]{1,0:T(8,128)(2,1)} %act_ref.5), channel_id=1, source_target_pairs={{0,16},{16,0},{1,17},{17,1},{2,18},{18,2},{3,19},{19,3},{4,20},{20... | collective-permute-start | bytes 3145736 | tf_op jit(solution)/shard_map/ppermute | solution.py:23
  23.2 0.7 broadcast_add_fusion
  23.9 1.2 convolution_convert_fusion
  25.1 1.9 %collective-permute-start.1 = (bf16[256,128]{1,0:T(8,128)(2,1)S(1)}, bf16[256,128]{1,0:T(8,128)(2,1)S(1)}, u32[]{:S(2)}, u32[]{:S(2)}) collective-permute-start(bf16[256,128]{1,0:T(8,128)(2,1)S(1)} %convolution_convert_fusion), channel_id=1, source_target_pairs={{0,16},{16,0},{1,17},{17,1},{2,18},{18,2},{3,19},{19,3},{4,20},{20... | collective-permute-start | bytes 196616 | tf_op jit(solution)/shard_map/ppermute | solution.py:23
  27.0 1.2 convolution_convert_fusion.1.keep_ref
  28.2 0.0 collective-permute-done.1.other_ref
  28.3 0.0 collective-permute-done.2.act_other_ref
  28.3 1.2 %copy-done = bf16[128,4096]{1,0:T(8,128)(2,1)S(1)} copy-done((bf16[128,4096]{1,0:T(8,128)(2,1)S(1)}, bf16[128,4096]{1,0:T(8,128)(2,1)}, u32[]{:S(2)}) %copy-start) | copy-done | bytes 1048600
  29.5 2.6 %shard_map.76 = bf16[4,2,64,2048]{3,2,1,0:T(8,128)(2,1)} custom-call(bf16[256,128]{1,0:T(8,128)(2,1)S(1)} %convolution_convert_fusion.1.keep_ref, bf16[256,128]{1,0:T(8,128)(2,1)S(1)} %collective-permute-done.1.other_ref, bf16[128,4096]{1,0:T(8,128)(2,1)S(1)} %copy-done, bf16[128,4096]{1,0:T(8,128)(2,1)S(1)} %collective-permute-done.2.act_other_ref), custom_call_target="tpu_custom_call" | custom-call | flops 536870912 | bytes 4194304 | tf_op jit(solution)/shard_map/pallas_call | solution.py:109
  32.0 3.7 %all-to-all-start = ((bf16[8,64,2048]{2,1,0:T(8,128)(2,1)}), bf16[8,64,2048]{2,1,0:T(8,128)(2,1)S(1)}, u32[]{:S(2)}, u32[]{:S(2)}) async-start(bf16[8,64,2048]{2,1,0:T(8,128)(2,1)} %bitcast.4), calls=%async_computation | async-start | bytes 4194304 | tf_op jit(solution)/shard_map/all_to_all | solution.py:122
  35.8 0.0 all-gather.2.cloned.1.call-start
  35.8 0.1 dynamic_slice.7
  35.9 0.1 multiply_convert_fusion
  36.1 7.8 %collective-permute-start = (bf16[128,512]{1,0:T(8,128)(2,1)S(1)}, bf16[128,512]{1,0:T(8,128)(2,1)S(1)}, u32[]{:S(2)}, u32[]{:S(2)}) collective-permute-start(bf16[128,512]{1,0:T(8,128)(2,1)S(1)} %reshape.28), channel_id=1, source_target_pairs={{0,1},{1,0},{2,3},{3,2},{4,5},{5,4},{6,7},{7,6},{8,9},{9,8},{10,11... | collective-permute-start | bytes 393224 | tf_op jit(solution)/shard_map/ppermute | solution.py:23
  43.9 7.4 %collective-permute-done = bf16[128,512]{1,0:T(8,128)(2,1)S(1)} collective-permute-done((bf16[128,512]{1,0:T(8,128)(2,1)S(1)}, bf16[128,512]{1,0:T(8,128)(2,1)S(1)}, u32[]{:S(2)}, u32[]{:S(2)}) %collective-permute-start) | collective-permute-done | bytes 131104 | tf_op jit(solution)/shard_map/ppermute | solution.py:23
  51.3 0.7 pad_maximum_fusion
  52.0 0.0 all-gather.2.cloned.1.call-update
  52.0 0.0 copy-start.1
  52.1 0.0 copy-start.3
  52.1 10.3 %all-to-all-done = bf16[8,64,2048]{2,1,0:T(8,128)(2,1)S(1)} async-done(((bf16[8,64,2048]{2,1,0:T(8,128)(2,1)}), bf16[8,64,2048]{2,1,0:T(8,128)(2,1)S(1)}, u32[]{:S(2)}, u32[]{:S(2)}) %all-to-all-start) | async-done | bytes 2097184 | tf_op jit(solution)/shard_map/all_to_all | solution.py:122
  62.3 0.4 reduce_sum.33
  62.7 0.2 reshape.30
  62.9 10.8 %all_to_all.15 = bf16[4,64,512]{2,1,0:T(8,128)(2,1)S(1)} all-to-all(bf16[4,64,512]{2,1,0:T(8,128)(2,1)S(1)} %copy.10), channel_id=1, replica_groups=mesh['x'=4,'l'=8,'c'=2,'Y'=4,'y'=2,'h'=2] {'Y'}, dimensions={0} | all-to-all | bytes 524288 | tf_op jit(solution)/shard_map/all_to_all | solution.py:126
  73.8 0.6 copy.11
  74.4 10.3 %all-to-all-start.2 = ((bf16[16,8,256]{2,1,0:T(8,128)(2,1)}), bf16[16,8,256]{2,1,0:T(8,128)(2,1)S(1)}, u32[]{:S(2)}, u32[]{:S(2)}) async-start(bf16[16,8,256]{2,1,0:T(8,128)(2,1)} %bitcast.7), calls=%async_computation.2 | async-start | bytes 131072 | tf_op jit(solution)/shard_map/all_to_all | solution.py:130
  84.7 17.4 %all-gather.2.cloned.1.call-done = bf16[2048,512]{1,0:T(8,128)(2,1)} async-done(((bf16[256,512]{1,0:T(8,128)(2,1)}), bf16[2048,512]{1,0:T(8,128)(2,1)}) %all-gather.2.cloned.1.call-update) | async-done | bytes 2097168 | tf_op jit(solution)/shard_map/all_gather | solution.py:120
  102.1 6.2 %collective-permute-start.3 = (bf16[2048,512]{1,0:T(8,128)(2,1)}, bf16[2048,512]{1,0:T(8,128)(2,1)S(1)}, u32[]{:S(2)}, u32[]{:S(2)}) collective-permute-start(bf16[2048,512]{1,0:T(8,128)(2,1)} %all-gather.2.cloned.1.call-done), channel_id=1, source_target_pairs={{0,16},{16,0},{1,17},{17,1},{2,18},{18,2},{3,19},{19,3},{4,20},{20... | collective-permute-start | bytes 6291464 | tf_op jit(solution)/shard_map/ppermute | solution.py:23
  108.2 0.1 pad_add_fusion.place
  108.3 1.6 %copy-done.2 = bf16[2048,512]{1,0:T(8,128)(2,1)S(1)} copy-done((bf16[2048,512]{1,0:T(8,128)(2,1)S(1)}, bf16[2048,512]{1,0:T(8,128)(2,1)}, u32[]{:S(2)}) %copy-start.2) | copy-done | bytes 2097176
  109.9 1.7 %shard_map.77 = (f32[128,512]{1,0:T(8,128)S(1)}, bf16[8,128,256]{2,1,0:T(8,128)(2,1)S(1)}) custom-call(s32[2]{0:T(128)S(1)} %pad_add_fusion.place, bf16[128,4096]{1,0:T(8,128)(2,1)S(1)} %copy-done.1, bf16[128,512]{1,0:T(8,128)(2,1)S(1)} %copy-done.3, bf16[8,2,128,512]{3,2,1,0:T(8,128)(2,1)S(1)} %bitcast.13), custom_call_target="tpu_custom_call" | custom-call | flops 536870912 | bytes 4194304 | tf_op jit(solution)/shard_map/pallas_call | solution.py:142
  111.6 0.6 convert_reduce_fusion
  112.2 2.7 %shard_map.78 = (bf16[128,512]{1,0:T(8,128)(2,1)}, bf16[128,4096]{1,0:T(8,128)(2,1)}) custom-call(s32[2]{0:T(128)S(1)} %pad_add_fusion.place, bf16[128,4096]{1,0:T(8,128)(2,1)S(1)} %copy-done.1, bf16[128,512]{1,0:T(8,128)(2,1)S(1)} %copy-done.3, bf16[8,2,128,512]{3,2,1,0:T(8,128)(2,1)S(1)} %bitcast.14, f32[128,512]{1,0:T(8,128)S(1)} %get-tuple-element.9.sum_ref, ...), custom_call_target="tpu_custom_call" | custom-call | flops 536870912 | bytes 4194304 | tf_op jit(solution)/shard_map/pallas_call | solution.py:142
  (14 shorter events, 0.2 us)
Async XLA Ops:
  7.2 21.1 %collective-permute-start.2 = (bf16[128,4096]{1,0:T(8,128)(2,1)}, bf16[128,4096]{1,0:T(8,128)(2,1)S(1)}, u32[]{:S(2)}, u32[]{:S(2)}) collective-permute-start(bf16[128,4096]{1,0:T(8,128)(2,1)} %act_ref.5), channel_id=1, source_target_pairs={{0,16},{16,0},{1,17},{17,1},{2,18},{18,2},{3,19},{19,3},{4,20},{20... | collective-permute-start | bytes 3145736 | tf_op jit(solution)/shard_map/ppermute | solution.py:23
  25.1 3.1 %collective-permute-start.1 = (bf16[256,128]{1,0:T(8,128)(2,1)S(1)}, bf16[256,128]{1,0:T(8,128)(2,1)S(1)}, u32[]{:S(2)}, u32[]{:S(2)}) collective-permute-start(bf16[256,128]{1,0:T(8,128)(2,1)S(1)} %convolution_convert_fusion), channel_id=1, source_target_pairs={{0,16},{16,0},{1,17},{17,1},{2,18},{18,2},{3,19},{19,3},{4,20},{20... | collective-permute-start | bytes 196616 | tf_op jit(solution)/shard_map/ppermute | solution.py:23
  28.3 1.2 %copy-start = (bf16[128,4096]{1,0:T(8,128)(2,1)S(1)}, bf16[128,4096]{1,0:T(8,128)(2,1)}, u32[]{:S(2)}) copy-start(bf16[128,4096]{1,0:T(8,128)(2,1)} %act_ref.5) | copy-start | bytes 3145732
  32.0 3.8 %copy-start.5 = (f32[64]{0:T(128)S(1)}, f32[64]{0:T(128)}, u32[]{:S(2)}) copy-start(f32[64]{0:T(128)} %param.7) | copy-start | bytes 772
  32.0 3.9 %copy-start.4 = (bf16[64,4,512]{2,1,0:T(4,128)(2,1)S(1)}, bf16[64,4,512]{2,1,0:T(4,128)(2,1)}, u32[]{:S(2)}) copy-start(bf16[64,4,512]{2,1,0:T(4,128)(2,1)} %param.6) | copy-start | bytes 786436
  32.0 30.3 %all-to-all-start = ((bf16[8,64,2048]{2,1,0:T(8,128)(2,1)}), bf16[8,64,2048]{2,1,0:T(8,128)(2,1)S(1)}, u32[]{:S(2)}, u32[]{:S(2)}) async-start(bf16[8,64,2048]{2,1,0:T(8,128)(2,1)} %bitcast.4), calls=%async_computation | async-start | bytes 4194304 | tf_op jit(solution)/shard_map/all_to_all | solution.py:122
  35.8 66.3 %all-gather.2.cloned.1.call-start = ((), (), s32[]{:S(2)}) async-start(), calls=%async_computation.3 | async-start | bytes 2359296 | tf_op jit(solution)/shard_map/all_gather | solution.py:120
  36.1 15.2 %collective-permute-start = (bf16[128,512]{1,0:T(8,128)(2,1)S(1)}, bf16[128,512]{1,0:T(8,128)(2,1)S(1)}, u32[]{:S(2)}, u32[]{:S(2)}) collective-permute-start(bf16[128,512]{1,0:T(8,128)(2,1)S(1)} %reshape.28), channel_id=1, source_target_pairs={{0,1},{1,0},{2,3},{3,2},{4,5},{5,4},{6,7},{7,6},{8,9},{9,8},{10,11... | collective-permute-start | bytes 393224 | tf_op jit(solution)/shard_map/ppermute | solution.py:23
  52.0 56.3 %copy-start.1 = (bf16[128,4096]{1,0:T(8,128)(2,1)S(1)}, bf16[128,4096]{1,0:T(8,128)(2,1)}, u32[]{:S(2)}) copy-start(bf16[128,4096]{1,0:T(8,128)(2,1)} %act_ref.5) | copy-start | bytes 3145732
  52.1 56.3 %copy-start.3 = (bf16[128,512]{1,0:T(8,128)(2,1)S(1)}, bf16[128,512]{1,0:T(8,128)(2,1)}, u32[]{:S(2)}) copy-start(bf16[128,512]{1,0:T(8,128)(2,1)} %cot_ref.3) | copy-start | bytes 393220
  74.4 27.6 %all-to-all-start.2 = ((bf16[16,8,256]{2,1,0:T(8,128)(2,1)}), bf16[16,8,256]{2,1,0:T(8,128)(2,1)S(1)}, u32[]{:S(2)}, u32[]{:S(2)}) async-start(bf16[16,8,256]{2,1,0:T(8,128)(2,1)} %bitcast.7), calls=%async_computation.2 | async-start | bytes 131072 | tf_op jit(solution)/shard_map/all_to_all | solution.py:130
  102.1 10.2 %collective-permute-start.3 = (bf16[2048,512]{1,0:T(8,128)(2,1)}, bf16[2048,512]{1,0:T(8,128)(2,1)S(1)}, u32[]{:S(2)}, u32[]{:S(2)}) collective-permute-start(bf16[2048,512]{1,0:T(8,128)(2,1)} %all-gather.2.cloned.1.call-done), channel_id=1, source_target_pairs={{0,16},{16,0},{1,17},{17,1},{2,18},{18,2},{3,19},{19,3},{4,20},{20... | collective-permute-start | bytes 6291464 | tf_op jit(solution)/shard_map/ppermute | solution.py:23
  108.3 1.6 %copy-start.2 = (bf16[2048,512]{1,0:T(8,128)(2,1)S(1)}, bf16[2048,512]{1,0:T(8,128)(2,1)}, u32[]{:S(2)}) copy-start(bf16[2048,512]{1,0:T(8,128)(2,1)} %all-gather.2.cloned.1.call-done) | copy-start | bytes 6291460
Sparse Core Ops, SparseCore 0:
  52.2 49.8 all-gather.1
